TPU v7x, 32 devices: a whole 2x2x4 slice. The times are simulated.
32 devices in a mesh: row: 8 (over y, x, core), col: 4 (over z).
Axes of the slice: x: 2, y: 2, z: 4, core: 2. Of those that a mesh axis runs over, the one named last changes fastest.
Arguments:
- features: bfloat16 [32, 1024, 1024], P(None, 'row', 'col'), may hold values from -45 to 45
- first_kernel: bfloat16 [3, 3, 32, 32], replicated, may hold values from -0.375 to 0.375
- second_kernel: bfloat16 [3, 3, 32, 32], replicated, may hold values from -0.375 to 0.375
- first_gain: float32 [32], replicated, may hold values from 0.5 to 1.5
- first_shift: float32 [32], replicated, may hold values from -3 to 3
- second_gain: float32 [32], replicated, may hold values from 0.5 to 1.5
- second_shift: float32 [32], replicated, may hold values from -3 to 3
Outputs:
- symmetric_map: bfloat16 [32, 1024, 1024], P(None, 'row', 'col')
All inputs are finite; a program needn't handle non-finite values.
Results may differ from a plain program's by a relative error of at most 0.0053.
Values may be sent and summed in bfloat16 or wider, within the bound.
A program may use at most 192 MiB of HBM per device.

v0:
```python
import jax
import jax.numpy as jnp
from jax import lax
from jax.sharding import PartitionSpec as P

DILATION_STEP = 8
epsilon = 1e-05


def with_halo(cells, sides, width):
    for axis, dim in sides:
        count = lax.axis_size(axis)
        ends = count - 1
        head = lax.slice_in_dim(cells, 0, width, axis=dim)
        tail = lax.slice_in_dim(cells, cells.shape[dim] - width, cells.shape[dim], axis=dim)
        cells = jnp.concatenate(
            [
                lax.ppermute(tail, axis, [(i, (i + 1) % count) for i in range(ends)]),
                cells,
                lax.ppermute(head, axis, [((i + 1) % count, i) for i in range(ends)]),
            ],
            axis=dim,
        )
    return cells


def apply_taps(padded, kernels, output_rows, output_columns):
    members = padded.shape[0]
    channels = kernels.shape[3]
    total = jnp.zeros((members, channels, output_rows, output_columns), jnp.float32)
    for filter_row in range(3):
        for filter_column in range(3):
            piece = padded[
                :,
                :,
                filter_row * DILATION_STEP : filter_row * DILATION_STEP + output_rows,
                filter_column * DILATION_STEP : filter_column * DILATION_STEP + output_columns,
            ]
            total = total + jnp.einsum(
                "poc,pchw->pohw",
                kernels[:, filter_row, filter_column],
                piece,
                preferred_element_type=jnp.float32,
            )
    return total


def extend(receptive_field):
    return with_halo(receptive_field, (("row", 2), ("col", 3)), DILATION_STEP)


def channel_affine(inner, gain, total_cells):
    sums = lax.psum(jnp.sum(inner, axis=(1, 2)), ("row", "col"))
    centre = sums / total_cells
    deviation = inner - centre[:, None, None]
    spread = lax.psum(jnp.sum(deviation * deviation, axis=(1, 2)), ("row", "col")) / total_cells
    factor = gain * lax.rsqrt(spread + epsilon)
    return (centre, factor)


def apply_norm(hidden, centre, factor, shift):
    return (hidden - centre[:, None, None]) * factor[:, None, None] + shift[:, None, None]


def residual_block(
    stacked, first_stack, second_stack, first_gain, first_shift, second_gain, second_shift
):
    tile_rows = stacked.shape[2]
    tile_cols = stacked.shape[3]
    row_devs = lax.axis_size("row")
    col_devs = lax.axis_size("col")
    total_cells = float(tile_rows * tile_cols * row_devs * col_devs)
    first = apply_taps(extend(stacked), first_stack, tile_rows, tile_cols)
    centre, factor = channel_affine(first[0], first_gain, total_cells)
    active = jnp.maximum(apply_norm(first, centre, factor, first_shift), 0.0).astype(jnp.bfloat16)
    second = apply_taps(extend(active), second_stack, tile_rows, tile_cols)
    centre_two, factor_two = channel_affine(second[0], second_gain, total_cells)
    return (
        stacked.astype(jnp.float32) + apply_norm(second, centre_two, factor_two, second_shift)
    ).astype(jnp.bfloat16)


def mirror(block):
    row_devs = lax.axis_size("row")
    col_devs = lax.axis_size("col")
    channels, tile_rows, tile_cols = block.shape
    ratio = row_devs // col_devs
    slab_rows = tile_rows // col_devs
    banded = lax.all_to_all(block, "col", split_axis=1, concat_axis=2, tiled=True)
    moved = lax.all_to_all(
        lax.all_to_all(banded, "row", split_axis=2, concat_axis=1, tiled=True),
        "col",
        split_axis=1,
        concat_axis=1,
        tiled=True,
    )
    arranged = moved.reshape(channels, col_devs, ratio, slab_rows, tile_rows)
    arranged = jnp.transpose(arranged, (0, 2, 1, 3, 4)).reshape(channels, tile_cols, tile_rows)
    return jnp.swapaxes(arranged, 1, 2)


def per_device(
    features, first_kernel, second_kernel, first_gain, first_shift, second_gain, second_shift
):
    summed = residual_block(
        features[None],
        first_kernel[None],
        second_kernel[None],
        first_gain,
        first_shift,
        second_gain,
        second_shift,
    )[0]
    total = summed.astype(jnp.float32) + mirror(summed).astype(jnp.float32)
    return (total * 0.5).astype(jnp.bfloat16)


def solution(mesh):
    placed = (P(None, "row", "col"), P(), P(), P(), P(), P(), P())
    return jax.shard_map(
        per_device, mesh=mesh, in_specs=placed, out_specs=P(None, "row", "col"), check_vma=False
    )
```

profile of v0, /device:TPU:0, one launch (start us, length us, event | category | flops | bytes accessed | tf_op | source)
XLA Modules:
  0.0 518.0 jit_solution(3476700549415977012)
XLA Ops:
  0.0 2.9 copy.68
  2.9 2.4 collective-permute-start
  5.3 1.3 collective-permute-start.1
  6.6 4.0 fusion.30
  11.0 1.6 fusion.38
  12.6 3.2 copy.40
  15.8 5.0 collective-permute-start.2
  20.8 2.1 copy.42
  22.8 1.5 collective-permute-start.3
  24.4 3.4 fusion.18
  27.7 3.4 fusion.26
  31.1 2.6 copy.41
  33.7 3.4 copy.43
  37.1 7.1 %pad_maximum_fusion = (bf16[1,32,144,264]{3,1,2,0:T(8,128)(2,1)S(1)}, bf16[1,32,144,264]{3,1,2,0:T(8,128)(2,1)S(1)}) fusion(bf16[1,32,144,8]{3,1,2,0:T(8,128)(2,1)} %copy.43, bf16[1,32,8,256]{3,1,2,0:T(8,128)(2,1)S(1)} %collective-permute-done.1, bf16[1,32,128,256]{3,1,2,0:T(8,128)(2,1)S(1)} %bitcast.206, ...), kind=kLoop, calls=%fused_computation.16 | loop fusion | flops 19464192 | bytes 7372800 | tf_op jit(solution)/shard_map/concatenate | solution.py:16
  44.2 2.6 fusion.21
  46.8 2.6 fusion.23
  49.5 2.8 fusion.22
  52.2 2.8 fusion.24
  55.0 2.8 fusion.29
  57.8 0.8 copy-done.5
  58.6 12.7 %fusion.41 = (f32[32]{0:T(128)S(1)}, f32[32,128,256]{2,0,1:T(8,128)}) fusion(bf16[1,32,144,264]{3,1,2,0:T(8,128)(2,1)S(1)} %get-tuple-element.9, bf16[1,3,3,32,32]{4,3,2,1,0:T(8,128)(2,1)} %bitcast.217, f32[128,256,32]{1,2,0:T(8,128)S(1)} %copy-done.5, f32[128,256,32]{1,2,0:T(8,128)} %fusion.21, f32[128,256,32]{1,2,0:T(8,128)} %fusion.22, ...), kind=kOutput, calls=%fused_computation.95 | convolution fusion | flops 76546016 | bytes 39854208 | tf_op jit(solution)/shard_map/poc,pchw->pohw/dot_general | solution.py:39
  71.3 43.9 %psum.28 = f32[32]{0:T(128)S(1)} all-reduce(f32[32]{0:T(128)S(1)} %get-tuple-element.17), channel_id=1, replica_groups=mesh['row'=8,'col'=4] {'row','col'}, use_global_device_ids=true, to_apply=%region_1.0 | all-reduce | flops 32 | bytes 256 | tf_op jit(solution)/shard_map/psum | solution.py:53
  115.2 2.8 multiply_reduce_fusion.1
  118.0 53.8 %psum.29 = f32[32]{0:T(128)S(1)} all-reduce(f32[32]{0:T(128)S(1)} %multiply_reduce_fusion.1), channel_id=1, replica_groups=mesh['row'=8,'col'=4] {'row','col'}, use_global_device_ids=true, to_apply=%region_3.0 | all-reduce | flops 32 | bytes 256 | tf_op jit(solution)/shard_map/psum | solution.py:56
  171.8 3.1 fusion.44
  175.0 1.3 collective-permute-start.4
  176.3 1.3 collective-permute-start.5
  177.6 3.5 fusion.32
  181.1 1.0 collective-permute-done.5
  182.3 1.6 fusion.37
  183.9 3.2 copy.45
  187.2 2.7 collective-permute-start.6
  189.9 2.1 copy.47
  192.0 1.3 collective-permute-start.7
  193.2 3.4 fusion.13
  196.6 3.3 fusion.5
  199.9 2.6 copy.46
  202.5 3.4 copy.48
  205.9 7.1 %pad_maximum_fusion.1 = (bf16[1,32,144,264]{3,1,2,0:T(8,128)(2,1)S(1)}, bf16[1,32,144,264]{3,1,2,0:T(8,128)(2,1)S(1)}) fusion(bf16[1,32,144,8]{3,1,2,0:T(8,128)(2,1)} %copy.48, bf16[1,32,8,256]{3,1,2,0:T(8,128)(2,1)S(1)} %collective-permute-done.5, bf16[1,32,128,256]{3,1,2,0:T(8,128)(2,1)S(1)} %fusion.44, ...), kind=kLoop, calls=%fused_computation.18 | loop fusion | flops 19464192 | bytes 7372800 | tf_op jit(solution)/shard_map/concatenate | solution.py:16
  213.1 2.6 fusion.10
  215.7 2.6 fusion.16
  218.3 2.6 fusion.8
  221.0 2.8 fusion.11
  223.7 2.8 fusion.9
  226.5 0.4 copy-done.6
  226.9 11.5 %fusion.42 = (f32[32]{0:T(128)S(1)}, f32[128,256,32]{1,2,0:T(8,128)}) fusion(bf16[1,32,144,264]{3,1,2,0:T(8,128)(2,1)S(1)} %get-tuple-element.5, bf16[1,3,3,32,32]{4,3,2,1,0:T(8,128)(2,1)} %bitcast.226, f32[128,256,32]{1,2,0:T(8,128)S(1)} %copy-done.7, f32[128,256,32]{1,2,0:T(8,128)} %fusion.8, f32[128,256,32]{1,2,0:T(8,128)} %fusion.9, ...), kind=kOutput, calls=%fused_computation.96 | convolution fusion | flops 76546016 | bytes 39854208 | tf_op jit(solution)/shard_map/poc,pchw->pohw/dot_general | solution.py:39
  238.5 43.7 %psum.30 = f32[32]{0:T(128)S(1)} all-reduce(f32[32]{0:T(128)S(1)} %get-tuple-element.19), channel_id=1, replica_groups=mesh['row'=8,'col'=4] {'row','col'}, use_global_device_ids=true, to_apply=%region_5.0 | all-reduce | flops 32 | bytes 256 | tf_op jit(solution)/shard_map/psum | solution.py:53
  282.2 2.8 multiply_reduce_fusion
  285.1 41.8 %psum.31 = f32[32]{0:T(128)S(1)} all-reduce(f32[32]{0:T(128)S(1)} %multiply_reduce_fusion), channel_id=1, replica_groups=mesh['row'=8,'col'=4] {'row','col'}, use_global_device_ids=true, to_apply=%region_7.0 | all-reduce | flops 32 | bytes 256 | tf_op jit(solution)/shard_map/psum | solution.py:56
  326.9 4.0 fusion.2
  330.9 50.7 %all_to_all.41 = bf16[32,128,256]{2,0,1:T(8,128)(2,1)S(1)} all-to-all(bf16[32,128,256]{2,0,1:T(8,128)(2,1)S(1)} %fusion.2), channel_id=1, replica_groups=mesh['row'=8,'col'=4] {'col'}, dimensions={1} | all-to-all | bytes 4194304 | tf_op jit(solution)/shard_map/all_to_all | solution.py:89
  381.6 1.6 copy.67
  383.3 7.1 %copy.58 = bf16[32,32,4,256]{1,0,3,2:T(8,128)(2,1)} copy(bf16[32,32,4,256]{3,2,1,0:T(4,128)(2,1)S(1)} %bitcast.210) | data formatting | bytes 4194304 | tf_op jit(solution)/shard_map/all_to_all | solution.py:89
  390.4 10.1 %reshape.252 = bf16[8,2,65536]{2,1,0:T(2,128)(2,1)S(1)} reshape(bf16[1024,32,32]{2,1,0:T(8,128)(2,1)} %bitcast.207) | data formatting | bytes 4194304
  400.5 30.1 %all_to_all.42 = bf16[8,2,65536]{2,1,0:T(2,128)(2,1)} all-to-all(bf16[8,2,65536]{2,1,0:T(2,128)(2,1)S(1)} %reshape.252), channel_id=1, replica_groups=mesh['row'=8,'col'=4] {'row'}, dimensions={0} | all-to-all | bytes 4194304 | tf_op jit(solution)/shard_map/all_to_all | solution.py:91
  430.6 8.7 %reshape.253 = bf16[1024,32,32]{2,1,0:T(8,128)(2,1)} reshape(bf16[8,2,65536]{2,1,0:T(2,128)(2,1)} %all_to_all.42) | data formatting | bytes 4194304
  439.3 12.6 %copy.61 = bf16[32,8,32,128]{3,0,2,1:T(8,128)(2,1)S(1)} copy(bf16[32,8,32,128]{2,0,3,1:T(8,128)(2,1)} %bitcast.208) | data formatting | bytes 4194304 | tf_op jit(solution)/shard_map/all_to_all | solution.py:91
  451.9 50.5 %all_to_all.43 = bf16[32,256,128]{2,0,1:T(8,128)(2,1)S(1)} all-to-all(bf16[32,256,128]{2,0,1:T(8,128)(2,1)S(1)} %bitcast.211), channel_id=1, replica_groups=mesh['row'=8,'col'=4] {'col'}, dimensions={1} | all-to-all | bytes 4194304 | tf_op jit(solution)/shard_map/all_to_all | solution.py:90
  502.4 0.8 copy.54
  503.2 0.6 convert_bitcast_fusion
  503.8 2.6 copy.55
  506.4 5.6 %copy.56 = f32[32,256,128]{1,0,2:T(8,128)} copy(f32[32,256,128]{2,1,0:T(8,128)} %bitcast.209) | data formatting | bytes 8388608 | tf_op jit(solution)/shard_map/convert_element_type | solution.py:114
  512.0 3.0 fusion.1
  515.1 2.5 copy.57
  (41 shorter events, 0.7 us)
Async XLA Ops:
  0.0 6.6 %copy-start.1 = (bf16[32,128,256]{2,1,0:T(8,128)(2,1)S(1)}, bf16[32,128,256]{2,1,0:T(8,128)(2,1)}, u32[]{:S(2)}) copy-start(bf16[32,128,256]{2,1,0:T(8,128)(2,1)} %param.7) | copy-start | bytes 6291460
  2.9 7.7 %collective-permute-start = (bf16[1,32,8,256]{3,1,2,0:T(8,128)(2,1)S(1)}, bf16[1,32,8,256]{3,1,2,0:T(8,128)(2,1)S(1)}, u32[]{:S(2)}, u32[]{:S(2)}) collective-permute-start(bf16[1,32,8,256]{3,1,2,0:T(8,128)(2,1)S(1)} %get-tuple-element.15), channel_id=1, source_target_pairs={{0,4},{4,8},{8,12},{12,16},{16,20},{20,24},{24,28},{1,5},{5,9},{9,... | collective-permute-start | bytes 393224 | tf_op jit(solution)/shard_map/ppermute | solution.py:18
  5.3 5.3 %collective-permute-start.1 = (bf16[1,32,8,256]{3,1,2,0:T(8,128)(2,1)S(1)}, bf16[1,32,8,256]{3,1,2,0:T(8,128)(2,1)S(1)}, u32[]{:S(2)}, u32[]{:S(2)}) collective-permute-start(bf16[1,32,8,256]{3,1,2,0:T(8,128)(2,1)S(1)} %get-tuple-element.16), channel_id=1, source_target_pairs={{4,0},{8,4},{12,8},{16,12},{20,16},{24,20},{28,24},{5,1},{9,5},{13... | collective-permute-start | bytes 393224 | tf_op jit(solution)/shard_map/ppermute | solution.py:20
  15.8 15.3 %collective-permute-start.2 = (bf16[1,32,144,8]{2,3,1,0:T(8,128)(2,1)}, bf16[1,32,144,8]{2,3,1,0:T(8,128)(2,1)}, u32[]{:S(2)}, u32[]{:S(2)}) collective-permute-start(bf16[1,32,144,8]{2,3,1,0:T(8,128)(2,1)} %copy.40), channel_id=1, source_target_pairs={{0,1},{1,2},{2,3},{4,5},{5,6},{6,7},{8,9},{9,10},{10,11},{12,13},{... | collective-permute-start | bytes 221192 | tf_op jit(solution)/shard_map/ppermute | solution.py:18
  22.8 10.8 %collective-permute-start.3 = (bf16[1,32,144,8]{2,3,1,0:T(8,128)(2,1)}, bf16[1,32,144,8]{2,3,1,0:T(8,128)(2,1)}, u32[]{:S(2)}, u32[]{:S(2)}) collective-permute-start(bf16[1,32,144,8]{2,3,1,0:T(8,128)(2,1)} %copy.42), channel_id=1, source_target_pairs={{1,0},{2,1},{3,2},{5,4},{6,5},{7,6},{9,8},{10,9},{11,10},{13,12},{... | collective-permute-start | bytes 221192 | tf_op jit(solution)/shard_map/ppermute | solution.py:20
  37.1 7.1 %copy-start.8 = (bf16[3,3,32,32]{3,2,1,0:T(8,128)(2,1)S(1)}, bf16[3,3,32,32]{3,2,1,0:T(8,128)(2,1)}, u32[]{:S(2)}) copy-start(bf16[3,3,32,32]{3,2,1,0:T(8,128)(2,1)} %param.8) | copy-start | bytes 55300
  55.0 3.6 copy-start.5
  71.3 100.5 %copy-start.12 = (f32[32]{0:T(128)S(1)}, f32[32]{0:T(128)}, u32[]{:S(2)}) copy-start(f32[32]{0:T(128)} %param.10) | copy-start | bytes 388
  71.3 100.5 %copy-start.10 = (f32[32]{0:T(128)S(1)}, f32[32]{0:T(128)}, u32[]{:S(2)}) copy-start(f32[32]{0:T(128)} %param.11) | copy-start | bytes 388
  171.8 5.8 %copy-start = (f32[32,128,256]{2,0,1:T(8,128)S(1)}, f32[32,128,256]{2,0,1:T(8,128)}, u32[]{:S(2)}) copy-start(f32[32,128,256]{2,0,1:T(8,128)} %get-tuple-element.18) | copy-start | bytes 12582916
  175.0 6.1 %collective-permute-start.4 = (bf16[1,32,8,256]{3,1,2,0:T(8,128)(2,1)S(1)}, bf16[1,32,8,256]{3,1,2,0:T(8,128)(2,1)S(1)}, u32[]{:S(2)}, u32[]{:S(2)}) collective-permute-start(bf16[1,32,8,256]{3,1,2,0:T(8,128)(2,1)S(1)} %get-tuple-element.13), channel_id=1, source_target_pairs={{0,4},{4,8},{8,12},{12,16},{16,20},{20,24},{24,28},{1,5},{5,9},{9,... | collective-permute-start | bytes 393224 | tf_op jit(solution)/shard_map/ppermute | solution.py:18
  176.3 5.7 %collective-permute-start.5 = (bf16[1,32,8,256]{3,1,2,0:T(8,128)(2,1)S(1)}, bf16[1,32,8,256]{3,1,2,0:T(8,128)(2,1)S(1)}, u32[]{:S(2)}, u32[]{:S(2)}) collective-permute-start(bf16[1,32,8,256]{3,1,2,0:T(8,128)(2,1)S(1)} %get-tuple-element.14), channel_id=1, source_target_pairs={{4,0},{8,4},{12,8},{16,12},{20,16},{24,20},{28,24},{5,1},{9,5},{13... | collective-permute-start | bytes 393224 | tf_op jit(solution)/shard_map/ppermute | solution.py:20
  187.2 12.7 %collective-permute-start.6 = (bf16[1,32,144,8]{2,3,1,0:T(8,128)(2,1)}, bf16[1,32,144,8]{2,3,1,0:T(8,128)(2,1)}, u32[]{:S(2)}, u32[]{:S(2)}) collective-permute-start(bf16[1,32,144,8]{2,3,1,0:T(8,128)(2,1)} %copy.45), channel_id=1, source_target_pairs={{0,1},{1,2},{2,3},{4,5},{5,6},{6,7},{8,9},{9,10},{10,11},{12,13},{... | collective-permute-start | bytes 221192 | tf_op jit(solution)/shard_map/ppermute | solution.py:18
  192.0 10.5 %collective-permute-start.7 = (bf16[1,32,144,8]{2,3,1,0:T(8,128)(2,1)}, bf16[1,32,144,8]{2,3,1,0:T(8,128)(2,1)}, u32[]{:S(2)}, u32[]{:S(2)}) collective-permute-start(bf16[1,32,144,8]{2,3,1,0:T(8,128)(2,1)} %copy.47), channel_id=1, source_target_pairs={{1,0},{2,1},{3,2},{5,4},{6,5},{7,6},{9,8},{10,9},{11,10},{13,12},{... | collective-permute-start | bytes 221192 | tf_op jit(solution)/shard_map/ppermute | solution.py:20
  205.9 7.1 %copy-start.9 = (bf16[3,3,32,32]{3,2,1,0:T(8,128)(2,1)S(1)}, bf16[3,3,32,32]{3,2,1,0:T(8,128)(2,1)}, u32[]{:S(2)}) copy-start(bf16[3,3,32,32]{3,2,1,0:T(8,128)(2,1)} %param.9) | copy-start | bytes 55300
  220.9 5.6 %copy-start.7 = (f32[128,256,32]{1,2,0:T(8,128)S(1)}, f32[128,256,32]{1,2,0:T(8,128)}, u32[]{:S(2)}) copy-start(f32[128,256,32]{1,2,0:T(8,128)} %fusion.5) | copy-start | bytes 12582916
  223.7 3.2 copy-start.6
  238.4 88.5 %copy-start.13 = (f32[32]{0:T(128)S(1)}, f32[32]{0:T(128)}, u32[]{:S(2)}) copy-start(f32[32]{0:T(128)} %param.12) | copy-start | bytes 388
  238.4 88.5 %copy-start.2 = (bf16[32,128,256]{2,1,0:T(8,128)(2,1)S(1)}, bf16[32,128,256]{2,1,0:T(8,128)(2,1)}, u32[]{:S(2)}) copy-start(bf16[32,128,256]{2,1,0:T(8,128)(2,1)} %param.7) | copy-start | bytes 6291460
  238.4 88.5 %copy-start.11 = (f32[32]{0:T(128)S(1)}, f32[32]{0:T(128)}, u32[]{:S(2)}) copy-start(f32[32]{0:T(128)} %param.13) | copy-start | bytes 388
  330.9 52.4 %copy-start.3 = (bf16[32,128,256]{2,0,1:T(8,128)(2,1)}, bf16[32,128,256]{2,0,1:T(8,128)(2,1)S(1)}, u32[]{:S(2)}) copy-start(bf16[32,128,256]{2,0,1:T(8,128)(2,1)S(1)} %fusion.2) | copy-start | bytes 6291460
  506.4 5.6 %copy-start.4 = (bf16[32,128,256]{2,0,1:T(8,128)(2,1)S(1)}, bf16[32,128,256]{2,0,1:T(8,128)(2,1)}, u32[]{:S(2)}) copy-start(bf16[32,128,256]{2,0,1:T(8,128)(2,1)} %copy-done.3) | copy-start | bytes 6291460
where the time goes:
time: 525 us; the launch traced here: 518 us
  blocking collectives  315 us (60%)
  local copies, waits for them, and re-layouts  81.8 us (16%)
  matrix products  72 us (14%)
  other arithmetic  31.2 us (6%)
  starting transfers between devices  16.7 us (3%)
    psum x2, blocking collectives, channel_affine(): lax.psum(jnp.sum(deviation * deviation, axis=(1, 2)), ('row', 'col'))  95.6 us
    psum x2, blocking collectives, channel_affine(): sums = lax.psum(jnp.sum(inner, axis=(1, 2)), ('row', 'col'))  87.6 us
    dot_general x18, matrix products, apply_taps(): jnp.einsum('poc,pchw->pohw', kernels[:, filter_row, filter_column], piece...  72 us
    all_to_all x1, blocking collectives, mirror(): lax.all_to_all(block, 'col', split_axis=1, concat_axis=2, tiled=True)  50.7 us
    all_to_all x1, blocking collectives, mirror(): lax.all_to_all(lax.all_to_all(banded, 'row', split_axis=2, concat_axis=1,...  50.5 us
    all_to_all x1, blocking collectives, mirror(): lax.all_to_all(banded, 'row', split_axis=2, concat_axis=1, tiled=True)  30.1 us
    unnamed x31, local copies, waits for them, and re-layouts  23.1 us
    concatenate x4, other arithmetic, with_halo(): jnp.concatenate([lax.ppermute(tail, axis, [(i, (i + 1) % count) for i in...  14.8 us
  transfers between devices with their start and end apart: 8, of which 1 were waited for; matrix products, arithmetic and copies ran while one was open for 6% of the time, Pallas kernels for 0%

commit v1 on v0

--- a/solution.py
+++ b/solution.py
@@ -50,7 +50,7 @@
 
 
 def channel_affine(inner, gain, total_cells):
-    sums = lax.psum(jnp.sum(inner, axis=(1, 2)), ("row", "col"))
+    sums = lax.psum(lax.psum(jnp.sum(inner, axis=(1, 2)), "col"), "row")
     centre = sums / total_cells
     deviation = inner - centre[:, None, None]
     spread = lax.psum(jnp.sum(deviation * deviation, axis=(1, 2)), ("row", "col")) / total_cells

time: 525 us -> 474 us (0.903)
  blocking collectives: 315 us -> 261 us
    psum x2 -> x4, blocking collectives: 87.6 us -> 52.5 us  [channel_affine(): sums = lax.psum(lax.psum(jnp.sum(inner, axis=(1, 2)), 'col'), 'row')]
    psum x2, blocking collectives: 95.6 us -> 75.8 us  [channel_affine(): lax.psum(jnp.sum(deviation * deviation, axis=(1, 2)), ('row', 'col'))]
where the time goes in v1:
time: 474 us; the launch traced here: 467 us
  blocking collectives  261 us (55%)
  local copies, waits for them, and re-layouts  81.7 us (17%)
  matrix products  72.1 us (15%)
  other arithmetic  31.2 us (7%)
  starting transfers between devices  19.7 us (4%)
    psum x2, blocking collectives, channel_affine(): lax.psum(jnp.sum(deviation * deviation, axis=(1, 2)), ('row', 'col'))  75.8 us
    dot_general x18, matrix products, apply_taps(): jnp.einsum('poc,pchw->pohw', kernels[:, filter_row, filter_column], piece...  72.1 us
    psum x4, blocking collectives, channel_affine(): sums = lax.psum(lax.psum(jnp.sum(inner, axis=(1, 2)), 'col'), 'row')  52.5 us
    all_to_all x1, blocking collectives, mirror(): lax.all_to_all(block, 'col', split_axis=1, concat_axis=2, tiled=True)  51.4 us
    all_to_all x1, blocking collectives, mirror(): lax.all_to_all(lax.all_to_all(banded, 'row', split_axis=2, concat_axis=1,...  50.5 us
    all_to_all x1, blocking collectives, mirror(): lax.all_to_all(banded, 'row', split_axis=2, concat_axis=1, tiled=True)  30.5 us
    unnamed x31, local copies, waits for them, and re-layouts  23 us
    concatenate x4, other arithmetic, with_halo(): jnp.concatenate([lax.ppermute(tail, axis, [(i, (i + 1) % count) for i in...  14.8 us
  transfers between devices with their start and end apart: 8, of which 1 were waited for; matrix products, arithmetic and copies ran while one was open for 6% of the time, Pallas kernels for 0%

profile of v1, /device:TPU:0, one launch (start us, length us, event | category | flops | bytes accessed | tf_op | source)
XLA Modules:
  0.0 467.1 jit_solution(9106376276695265468)
XLA Ops:
  0.0 2.9 copy.68
  2.9 2.4 collective-permute-start
  5.3 1.3 collective-permute-start.1
  6.6 4.0 fusion.30
  11.0 1.6 fusion.38
  12.6 3.2 copy.40
  15.8 4.9 %collective-permute-start.2 = (bf16[1,32,144,8]{2,3,1,0:T(8,128)(2,1)}, bf16[1,32,144,8]{2,3,1,0:T(8,128)(2,1)}, u32[]{:S(2)}, u32[]{:S(2)}) collective-permute-start(bf16[1,32,144,8]{2,3,1,0:T(8,128)(2,1)} %copy.40), channel_id=1, source_target_pairs={{0,1},{1,2},{2,3},{4,5},{5,6},{6,7},{8,9},{9,10},{10,11},{12,13},{... | collective-permute-start | bytes 221192 | tf_op jit(solution)/shard_map/ppermute | solution.py:18
  20.7 2.1 copy.42
  22.8 1.8 collective-permute-start.3
  24.6 3.4 fusion.18
  28.0 3.3 fusion.26
  31.3 2.6 copy.41
  33.9 3.4 copy.43
  37.3 7.1 %pad_maximum_fusion = (bf16[1,32,144,264]{3,1,2,0:T(8,128)(2,1)S(1)}, bf16[1,32,144,264]{3,1,2,0:T(8,128)(2,1)S(1)}) fusion(bf16[1,32,144,8]{3,1,2,0:T(8,128)(2,1)} %copy.43, bf16[1,32,8,256]{3,1,2,0:T(8,128)(2,1)S(1)} %collective-permute-done.1, bf16[1,32,128,256]{3,1,2,0:T(8,128)(2,1)S(1)} %bitcast.206, ...), kind=kLoop, calls=%fused_computation.16 | loop fusion | flops 19464192 | bytes 7372800 | tf_op jit(solution)/shard_map/concatenate | solution.py:16
  44.5 2.7 fusion.21
  47.1 2.6 fusion.23
  49.7 2.8 fusion.22
  52.5 2.8 fusion.24
  55.3 2.8 fusion.29
  58.1 0.8 copy-done.5
  58.9 12.7 %fusion.41 = (f32[32]{0:T(128)S(1)}, f32[32,128,256]{2,0,1:T(8,128)}) fusion(bf16[1,32,144,264]{3,1,2,0:T(8,128)(2,1)S(1)} %get-tuple-element.9, bf16[1,3,3,32,32]{4,3,2,1,0:T(8,128)(2,1)} %bitcast.217, f32[128,256,32]{1,2,0:T(8,128)S(1)} %copy-done.5, f32[128,256,32]{1,2,0:T(8,128)} %fusion.21, f32[128,256,32]{1,2,0:T(8,128)} %fusion.22, ...), kind=kOutput, calls=%fused_computation.95 | convolution fusion | flops 76546016 | bytes 39854208 | tf_op jit(solution)/shard_map/poc,pchw->pohw/dot_general | solution.py:39
  71.6 13.0 %psum.42 = f32[32]{0:T(128)S(1)} all-reduce(f32[32]{0:T(128)S(1)} %get-tuple-element.17), channel_id=1, replica_groups=mesh['row'=8,'col'=4] {'col'}, use_global_device_ids=true, to_apply=%region_1.0 | all-reduce | flops 32 | bytes 256 | tf_op jit(solution)/shard_map/psum | solution.py:53
  84.6 13.7 %psum.43 = f32[32]{0:T(128)S(1)} all-reduce(f32[32]{0:T(128)S(1)} %psum.42), channel_id=1, replica_groups=mesh['row'=8,'col'=4] {'row'}, use_global_device_ids=true, to_apply=%region_2.0 | all-reduce | flops 32 | bytes 256 | tf_op jit(solution)/shard_map/psum | solution.py:53
  98.3 2.8 multiply_reduce_fusion.1
  101.2 38.1 %psum.44 = f32[32]{0:T(128)S(1)} all-reduce(f32[32]{0:T(128)S(1)} %multiply_reduce_fusion.1), channel_id=1, replica_groups=mesh['row'=8,'col'=4] {'row','col'}, use_global_device_ids=true, to_apply=%region_4.0 | all-reduce | flops 32 | bytes 256 | tf_op jit(solution)/shard_map/psum | solution.py:56
  139.3 3.1 fusion.44
  142.4 1.3 collective-permute-start.4
  143.7 1.3 collective-permute-start.5
  145.0 3.5 fusion.32
  148.5 1.0 collective-permute-done.5
  149.8 1.6 fusion.37
  151.4 3.2 copy.45
  154.6 5.4 %collective-permute-start.6 = (bf16[1,32,144,8]{2,3,1,0:T(8,128)(2,1)}, bf16[1,32,144,8]{2,3,1,0:T(8,128)(2,1)}, u32[]{:S(2)}, u32[]{:S(2)}) collective-permute-start(bf16[1,32,144,8]{2,3,1,0:T(8,128)(2,1)} %copy.45), channel_id=1, source_target_pairs={{0,1},{1,2},{2,3},{4,5},{5,6},{6,7},{8,9},{9,10},{10,11},{12,13},{... | collective-permute-start | bytes 221192 | tf_op jit(solution)/shard_map/ppermute | solution.py:18
  160.0 2.1 copy.47
  162.1 1.3 collective-permute-start.7
  163.4 3.3 fusion.13
  166.7 3.3 fusion.5
  170.1 2.6 copy.46
  172.7 3.4 copy.48
  176.1 7.1 %pad_maximum_fusion.1 = (bf16[1,32,144,264]{3,1,2,0:T(8,128)(2,1)S(1)}, bf16[1,32,144,264]{3,1,2,0:T(8,128)(2,1)S(1)}) fusion(bf16[1,32,144,8]{3,1,2,0:T(8,128)(2,1)} %copy.48, bf16[1,32,8,256]{3,1,2,0:T(8,128)(2,1)S(1)} %collective-permute-done.5, bf16[1,32,128,256]{3,1,2,0:T(8,128)(2,1)S(1)} %fusion.44, ...), kind=kLoop, calls=%fused_computation.18 | loop fusion | flops 19464192 | bytes 7372800 | tf_op jit(solution)/shard_map/concatenate | solution.py:16
  183.2 2.7 fusion.10
  185.9 2.6 fusion.16
  188.5 2.6 fusion.8
  191.1 2.8 fusion.11
  193.9 2.8 fusion.9
  197.1 11.5 %fusion.42 = (f32[32]{0:T(128)S(1)}, f32[128,256,32]{1,2,0:T(8,128)}) fusion(bf16[1,32,144,264]{3,1,2,0:T(8,128)(2,1)S(1)} %get-tuple-element.5, bf16[1,3,3,32,32]{4,3,2,1,0:T(8,128)(2,1)} %bitcast.226, f32[128,256,32]{1,2,0:T(8,128)S(1)} %copy-done.7, f32[128,256,32]{1,2,0:T(8,128)} %fusion.8, f32[128,256,32]{1,2,0:T(8,128)} %fusion.9, ...), kind=kOutput, calls=%fused_computation.96 | convolution fusion | flops 76546016 | bytes 39854208 | tf_op jit(solution)/shard_map/poc,pchw->pohw/dot_general | solution.py:39
  208.6 11.1 %psum.45 = f32[32]{0:T(128)S(1)} all-reduce(f32[32]{0:T(128)S(1)} %get-tuple-element.19), channel_id=1, replica_groups=mesh['row'=8,'col'=4] {'col'}, use_global_device_ids=true, to_apply=%region_6.0 | all-reduce | flops 32 | bytes 256 | tf_op jit(solution)/shard_map/psum | solution.py:53
  219.8 14.5 %psum.46 = f32[32]{0:T(128)S(1)} all-reduce(f32[32]{0:T(128)S(1)} %psum.45), channel_id=1, replica_groups=mesh['row'=8,'col'=4] {'row'}, use_global_device_ids=true, to_apply=%region_7.0 | all-reduce | flops 32 | bytes 256 | tf_op jit(solution)/shard_map/psum | solution.py:53
  234.3 2.8 multiply_reduce_fusion
  237.2 37.7 %psum.47 = f32[32]{0:T(128)S(1)} all-reduce(f32[32]{0:T(128)S(1)} %multiply_reduce_fusion), channel_id=1, replica_groups=mesh['row'=8,'col'=4] {'row','col'}, use_global_device_ids=true, to_apply=%region_9.0 | all-reduce | flops 32 | bytes 256 | tf_op jit(solution)/shard_map/psum | solution.py:56
  274.9 4.0 fusion.2
  278.9 51.4 %all_to_all.41 = bf16[32,128,256]{2,0,1:T(8,128)(2,1)S(1)} all-to-all(bf16[32,128,256]{2,0,1:T(8,128)(2,1)S(1)} %fusion.2), channel_id=1, replica_groups=mesh['row'=8,'col'=4] {'col'}, dimensions={1} | all-to-all | bytes 4194304 | tf_op jit(solution)/shard_map/all_to_all | solution.py:89
  330.3 1.6 copy.67
  331.9 7.1 %copy.58 = bf16[32,32,4,256]{1,0,3,2:T(8,128)(2,1)} copy(bf16[32,32,4,256]{3,2,1,0:T(4,128)(2,1)S(1)} %bitcast.210) | data formatting | bytes 4194304 | tf_op jit(solution)/shard_map/all_to_all | solution.py:89
  339.0 10.1 %reshape.252 = bf16[8,2,65536]{2,1,0:T(2,128)(2,1)S(1)} reshape(bf16[1024,32,32]{2,1,0:T(8,128)(2,1)} %bitcast.207) | data formatting | bytes 4194304
  349.2 30.5 %all_to_all.42 = bf16[8,2,65536]{2,1,0:T(2,128)(2,1)} all-to-all(bf16[8,2,65536]{2,1,0:T(2,128)(2,1)S(1)} %reshape.252), channel_id=1, replica_groups=mesh['row'=8,'col'=4] {'row'}, dimensions={0} | all-to-all | bytes 4194304 | tf_op jit(solution)/shard_map/all_to_all | solution.py:91
  379.7 8.7 %reshape.253 = bf16[1024,32,32]{2,1,0:T(8,128)(2,1)} reshape(bf16[8,2,65536]{2,1,0:T(2,128)(2,1)} %all_to_all.42) | data formatting | bytes 4194304
  388.4 12.6 %copy.61 = bf16[32,8,32,128]{3,0,2,1:T(8,128)(2,1)S(1)} copy(bf16[32,8,32,128]{2,0,3,1:T(8,128)(2,1)} %bitcast.208) | data formatting | bytes 4194304 | tf_op jit(solution)/shard_map/all_to_all | solution.py:91
  400.9 50.5 %all_to_all.43 = bf16[32,256,128]{2,0,1:T(8,128)(2,1)S(1)} all-to-all(bf16[32,256,128]{2,0,1:T(8,128)(2,1)S(1)} %bitcast.211), channel_id=1, replica_groups=mesh['row'=8,'col'=4] {'col'}, dimensions={1} | all-to-all | bytes 4194304 | tf_op jit(solution)/shard_map/all_to_all | solution.py:90
  451.5 0.8 copy.54
  452.9 2.6 copy.55
  455.5 5.6 %copy.56 = f32[32,256,128]{1,0,2:T(8,128)} copy(f32[32,256,128]{2,1,0:T(8,128)} %bitcast.209) | data formatting | bytes 8388608 | tf_op jit(solution)/shard_map/convert_element_type | solution.py:114
  461.1 3.0 fusion.1
  464.1 2.5 copy.57
  (43 shorter events, 1.7 us)
Async XLA Ops:
  0.0 6.6 %copy-start.1 = (bf16[32,128,256]{2,1,0:T(8,128)(2,1)S(1)}, bf16[32,128,256]{2,1,0:T(8,128)(2,1)}, u32[]{:S(2)}) copy-start(bf16[32,128,256]{2,1,0:T(8,128)(2,1)} %param.7) | copy-start | bytes 6291460
  2.9 7.7 %collective-permute-start = (bf16[1,32,8,256]{3,1,2,0:T(8,128)(2,1)S(1)}, bf16[1,32,8,256]{3,1,2,0:T(8,128)(2,1)S(1)}, u32[]{:S(2)}, u32[]{:S(2)}) collective-permute-start(bf16[1,32,8,256]{3,1,2,0:T(8,128)(2,1)S(1)} %get-tuple-element.15), channel_id=1, source_target_pairs={{0,4},{4,8},{8,12},{12,16},{16,20},{20,24},{24,28},{1,5},{5,9},{9,... | collective-permute-start | bytes 393224 | tf_op jit(solution)/shard_map/ppermute | solution.py:18
  5.3 5.3 %collective-permute-start.1 = (bf16[1,32,8,256]{3,1,2,0:T(8,128)(2,1)S(1)}, bf16[1,32,8,256]{3,1,2,0:T(8,128)(2,1)S(1)}, u32[]{:S(2)}, u32[]{:S(2)}) collective-permute-start(bf16[1,32,8,256]{3,1,2,0:T(8,128)(2,1)S(1)} %get-tuple-element.16), channel_id=1, source_target_pairs={{4,0},{8,4},{12,8},{16,12},{20,16},{24,20},{28,24},{5,1},{9,5},{13... | collective-permute-start | bytes 393224 | tf_op jit(solution)/shard_map/ppermute | solution.py:20
  15.8 15.5 %collective-permute-start.2 = (bf16[1,32,144,8]{2,3,1,0:T(8,128)(2,1)}, bf16[1,32,144,8]{2,3,1,0:T(8,128)(2,1)}, u32[]{:S(2)}, u32[]{:S(2)}) collective-permute-start(bf16[1,32,144,8]{2,3,1,0:T(8,128)(2,1)} %copy.40), channel_id=1, source_target_pairs={{0,1},{1,2},{2,3},{4,5},{5,6},{6,7},{8,9},{9,10},{10,11},{12,13},{... | collective-permute-start | bytes 221192 | tf_op jit(solution)/shard_map/ppermute | solution.py:18
  22.8 11.1 %collective-permute-start.3 = (bf16[1,32,144,8]{2,3,1,0:T(8,128)(2,1)}, bf16[1,32,144,8]{2,3,1,0:T(8,128)(2,1)}, u32[]{:S(2)}, u32[]{:S(2)}) collective-permute-start(bf16[1,32,144,8]{2,3,1,0:T(8,128)(2,1)} %copy.42), channel_id=1, source_target_pairs={{1,0},{2,1},{3,2},{5,4},{6,5},{7,6},{9,8},{10,9},{11,10},{13,12},{... | collective-permute-start | bytes 221192 | tf_op jit(solution)/shard_map/ppermute | solution.py:20
  37.3 7.1 %copy-start.8 = (bf16[3,3,32,32]{3,2,1,0:T(8,128)(2,1)S(1)}, bf16[3,3,32,32]{3,2,1,0:T(8,128)(2,1)}, u32[]{:S(2)}) copy-start(bf16[3,3,32,32]{3,2,1,0:T(8,128)(2,1)} %param.8) | copy-start | bytes 55300
  55.3 3.6 copy-start.5
  71.5 67.7 %copy-start.12 = (f32[32]{0:T(128)S(1)}, f32[32]{0:T(128)}, u32[]{:S(2)}) copy-start(f32[32]{0:T(128)} %param.10) | copy-start | bytes 388
  71.5 67.7 %copy-start.10 = (f32[32]{0:T(128)S(1)}, f32[32]{0:T(128)}, u32[]{:S(2)}) copy-start(f32[32]{0:T(128)} %param.11) | copy-start | bytes 388
  139.2 5.8 %copy-start = (f32[32,128,256]{2,0,1:T(8,128)S(1)}, f32[32,128,256]{2,0,1:T(8,128)}, u32[]{:S(2)}) copy-start(f32[32,128,256]{2,0,1:T(8,128)} %get-tuple-element.18) | copy-start | bytes 12582916
  142.4 6.1 %collective-permute-start.4 = (bf16[1,32,8,256]{3,1,2,0:T(8,128)(2,1)S(1)}, bf16[1,32,8,256]{3,1,2,0:T(8,128)(2,1)S(1)}, u32[]{:S(2)}, u32[]{:S(2)}) collective-permute-start(bf16[1,32,8,256]{3,1,2,0:T(8,128)(2,1)S(1)} %get-tuple-element.13), channel_id=1, source_target_pairs={{0,4},{4,8},{8,12},{12,16},{16,20},{20,24},{24,28},{1,5},{5,9},{9,... | collective-permute-start | bytes 393224 | tf_op jit(solution)/shard_map/ppermute | solution.py:18
  143.7 5.7 %collective-permute-start.5 = (bf16[1,32,8,256]{3,1,2,0:T(8,128)(2,1)S(1)}, bf16[1,32,8,256]{3,1,2,0:T(8,128)(2,1)S(1)}, u32[]{:S(2)}, u32[]{:S(2)}) collective-permute-start(bf16[1,32,8,256]{3,1,2,0:T(8,128)(2,1)S(1)} %get-tuple-element.14), channel_id=1, source_target_pairs={{4,0},{8,4},{12,8},{16,12},{20,16},{24,20},{28,24},{5,1},{9,5},{13... | collective-permute-start | bytes 393224 | tf_op jit(solution)/shard_map/ppermute | solution.py:20
  154.6 15.4 %collective-permute-start.6 = (bf16[1,32,144,8]{2,3,1,0:T(8,128)(2,1)}, bf16[1,32,144,8]{2,3,1,0:T(8,128)(2,1)}, u32[]{:S(2)}, u32[]{:S(2)}) collective-permute-start(bf16[1,32,144,8]{2,3,1,0:T(8,128)(2,1)} %copy.45), channel_id=1, source_target_pairs={{0,1},{1,2},{2,3},{4,5},{5,6},{6,7},{8,9},{9,10},{10,11},{12,13},{... | collective-permute-start | bytes 221192 | tf_op jit(solution)/shard_map/ppermute | solution.py:18
  162.1 10.5 %collective-permute-start.7 = (bf16[1,32,144,8]{2,3,1,0:T(8,128)(2,1)}, bf16[1,32,144,8]{2,3,1,0:T(8,128)(2,1)}, u32[]{:S(2)}, u32[]{:S(2)}) collective-permute-start(bf16[1,32,144,8]{2,3,1,0:T(8,128)(2,1)} %copy.47), channel_id=1, source_target_pairs={{1,0},{2,1},{3,2},{5,4},{6,5},{7,6},{9,8},{10,9},{11,10},{13,12},{... | collective-permute-start | bytes 221192 | tf_op jit(solution)/shard_map/ppermute | solution.py:20
  176.1 7.1 %copy-start.9 = (bf16[3,3,32,32]{3,2,1,0:T(8,128)(2,1)S(1)}, bf16[3,3,32,32]{3,2,1,0:T(8,128)(2,1)}, u32[]{:S(2)}) copy-start(bf16[3,3,32,32]{3,2,1,0:T(8,128)(2,1)} %param.9) | copy-start | bytes 55300
  191.1 5.6 %copy-start.7 = (f32[128,256,32]{1,2,0:T(8,128)S(1)}, f32[128,256,32]{1,2,0:T(8,128)}, u32[]{:S(2)}) copy-start(f32[128,256,32]{1,2,0:T(8,128)} %fusion.5) | copy-start | bytes 12582916
  193.9 3.2 copy-start.6
  208.6 66.3 %copy-start.13 = (f32[32]{0:T(128)S(1)}, f32[32]{0:T(128)}, u32[]{:S(2)}) copy-start(f32[32]{0:T(128)} %param.12) | copy-start | bytes 388
  208.6 66.3 %copy-start.2 = (bf16[32,128,256]{2,1,0:T(8,128)(2,1)S(1)}, bf16[32,128,256]{2,1,0:T(8,128)(2,1)}, u32[]{:S(2)}) copy-start(bf16[32,128,256]{2,1,0:T(8,128)(2,1)} %param.7) | copy-start | bytes 6291460
  208.6 66.3 %copy-start.11 = (f32[32]{0:T(128)S(1)}, f32[32]{0:T(128)}, u32[]{:S(2)}) copy-start(f32[32]{0:T(128)} %param.13) | copy-start | bytes 388
  278.9 53.0 %copy-start.3 = (bf16[32,128,256]{2,0,1:T(8,128)(2,1)}, bf16[32,128,256]{2,0,1:T(8,128)(2,1)S(1)}, u32[]{:S(2)}) copy-start(bf16[32,128,256]{2,0,1:T(8,128)(2,1)S(1)} %fusion.2) | copy-start | bytes 6291460
  455.5 5.7 %copy-start.4 = (bf16[32,128,256]{2,0,1:T(8,128)(2,1)S(1)}, bf16[32,128,256]{2,0,1:T(8,128)(2,1)}, u32[]{:S(2)}) copy-start(bf16[32,128,256]{2,0,1:T(8,128)(2,1)} %copy-done.3) | copy-start | bytes 6291460
